TPU v7x, 256 devices: a whole 4x4x8 slice. The times are simulated.
256 devices in a mesh: seq: 64 (over z, y, core), head: 4 (over x).
Axes of the slice: x: 4, y: 4, z: 8, core: 2. Of those that a mesh axis runs over, the one named last changes fastest.
Arguments:
- queries: bfloat16 [65536, 5120], P('seq', 'head'), may hold values from -96 to 96
- keys: bfloat16 [65536, 5120], P('seq', 'head'), may hold values from -4.5 to 4.5
- values: bfloat16 [65536, 5120], P('seq', 'head'), may hold values from -6 to 6
- head_class: int32 [40], P('head'), may hold values from 0 to 1, as said below
- mask_spatial: int32 [64, 8, 8], P('seq'), may hold values from 0 to 1, as said below
- mask_temporal: int32 [256, 2, 2], P('seq'), may hold values from 0 to 1, as said below
Outputs:
- attended: bfloat16 [65536, 5120], P('seq', 'head')
Inputs may be any that keep to these rules, and one draw needn't show every extreme that they name: `head_class`: each aligned block of 10 heads holds exactly 4 temporal heads. `mask_spatial`: every diagonal tile is 1. `mask_temporal`: every diagonal tile is 1.
All inputs are finite; a program needn't handle non-finite values.
Results may differ from a plain program's by a relative error of at most 0.0044.
Values may be sent and summed in bfloat16 or wider, within the bound.
A program may use at most 128 MiB of HBM per device.

v0:
```python
import jax
import jax.numpy as jnp
from jax import lax
from jax.sharding import PartitionSpec as P

HEAD_DIM = 128
HT_DEV = 4


def shortened(value):

    def short(part):
        return part.astype(jnp.bfloat16) if part.dtype == jnp.float32 else part

    return jax.tree.map(short, value)


def widen_mask(mask):
    allowed = mask > 0
    return jnp.repeat(jnp.repeat(allowed, 128, axis=1), 128, axis=2)


def attend(query, key_rows, value_rows, allowed):
    scores = jnp.einsum("bqhd,bkhd->bhqk", query, key_rows, preferred_element_type=jnp.float32)
    scores = scores * query.shape[-1] ** (-0.5)
    scores = jnp.where(allowed[:, None], scores, -1e30)
    top = jnp.max(scores, axis=-1, keepdims=True)
    weights = jnp.exp(scores - top)
    total = jnp.sum(weights, axis=-1, keepdims=True)
    mixed = (
        jnp.einsum(
            "bhqk,bkhd->bhqd",
            weights.astype(jnp.bfloat16),
            value_rows,
            preferred_element_type=jnp.float32,
        )
        / total
    )
    return jnp.transpose(mixed, (0, 2, 1, 3)).astype(jnp.bfloat16)


def on_device(queries, keys, values, head_class, mask_spatial, mask_temporal):
    rows = queries.shape[0]
    local_heads = queries.shape[1] // HEAD_DIM
    seq_count = lax.axis_size("seq")
    head_count = lax.axis_size("head")
    group_rows = rows // (seq_count * head_count)
    order = jnp.argsort(1 - head_class, stable=True)
    chosen_t = order[:HT_DEV]
    chosen_s = order[HT_DEV:]
    shaped = [a.reshape(rows, local_heads, HEAD_DIM) for a in (queries, keys, values)]
    spatial = [jnp.take(a, chosen_s, axis=1) for a in shaped]
    temporal = [jnp.take(a, chosen_t, axis=1) for a in shaped]
    parts = tuple(
        (a.reshape(1, seq_count, head_count, group_rows, HT_DEV, HEAD_DIM) for a in temporal)
    )
    moved = jax.tree.map(
        lambda part, own: part.astype(own.dtype),
        lax.all_to_all(
            lax.all_to_all(shortened(parts), "seq", split_axis=1, concat_axis=0, tiled=True),
            "head",
            split_axis=2,
            concat_axis=4,
            tiled=True,
        ),
        parts,
    )
    wide_heads = head_count * HT_DEV
    blocks = [
        jnp.transpose(a.reshape(seq_count, group_rows, wide_heads, HEAD_DIM), (1, 0, 2, 3)).reshape(
            1, group_rows * seq_count, wide_heads, HEAD_DIM
        )
        for a in moved
    ]
    own_mask = lax.dynamic_slice_in_dim(mask_temporal, lax.axis_index("head"), 1, 0)
    result = attend(blocks[0], blocks[1], blocks[2], widen_mask(own_mask))
    back = jnp.transpose(result.reshape(group_rows, seq_count, wide_heads, HEAD_DIM), (1, 0, 2, 3))
    back = back.reshape(seq_count, 1, 1, group_rows, wide_heads, HEAD_DIM)
    back = lax.all_to_all(
        lax.all_to_all(back, "seq", split_axis=0, concat_axis=1, tiled=True),
        "head",
        split_axis=4,
        concat_axis=2,
        tiled=True,
    )
    temporal_out = back.reshape(rows, HT_DEV, HEAD_DIM)
    spatial_out = attend(
        spatial[0][None], spatial[1][None], spatial[2][None], widen_mask(mask_spatial)
    )[0]
    joined = jnp.concatenate([temporal_out, spatial_out], axis=1)
    restored = jnp.take(joined, jnp.argsort(order), axis=1)
    return restored.reshape(rows, local_heads * HEAD_DIM)


def solution(mesh):
    return jax.shard_map(
        on_device,
        mesh=mesh,
        in_specs=(
            P("seq", "head"),
            P("seq", "head"),
            P("seq", "head"),
            P("head"),
            P("seq", None, None),
            P("seq", None, None),
        ),
        out_specs=P("seq", "head"),
        check_vma=False,
    )
```

profile of v0, /device:TPU:1, one launch (start us, length us, event | category | flops | bytes accessed | tf_op | source)
XLA Modules:
  0.0 282.9 jit_solution(15514275125762515269)
XLA Ops:
  0.7 1.3 sort.34
  1.9 4.4 %copy.33 = bf16[1024,1280]{0,1:T(8,128)(2,1)} copy(bf16[1024,1280]{1,0:T(8,128)(2,1)} %param.10) | data formatting | bytes 5242880 | tf_op args[0]
  6.3 3.2 %copy.34 = bf16[1024,10,128]{2,0,1:T(8,128)(2,1)S(1)} copy(bf16[1024,10,128]{0,2,1:T(8,128)(2,1)} %bitcast.98) | data formatting | bytes 5242880 | tf_op jit(solution)/shard_map/reshape | solution.py:51
  9.6 4.9 %copy.38 = bf16[1024,1280]{0,1:T(8,128)(2,1)} copy(bf16[1024,1280]{1,0:T(8,128)(2,1)} %param.11) | data formatting | bytes 5242880 | tf_op args[1]
  14.5 4.4 %copy.39 = bf16[1024,10,128]{2,0,1:T(8,128)(2,1)} copy(bf16[1024,10,128]{0,2,1:T(8,128)(2,1)} %bitcast.99) | data formatting | bytes 5242880 | tf_op jit(solution)/shard_map/reshape | solution.py:51
  18.9 1.7 gather_fusion.1
  20.6 3.5 %gather_fusion.2 = bf16[4,1024,128]{2,1,0:T(8,128)(2,1)} fusion(bf16[1024,10,128]{2,0,1:T(8,128)(2,1)} %copy.39, s32[1024]{0:T(1024)S(1)} %pad_clamp_fusion.2), kind=kCustom, calls=%fused_computation.2.clone | custom fusion | bytes 2097168 | tf_op jit(solution)/shard_map/jit(_take)/gather | solution.py:53
  24.1 4.4 %copy.43 = bf16[1024,1280]{0,1:T(8,128)(2,1)} copy(bf16[1024,1280]{1,0:T(8,128)(2,1)} %param.12) | data formatting | bytes 5242880 | tf_op args[2]
  28.5 3.2 %copy.44 = bf16[1024,10,128]{2,0,1:T(8,128)(2,1)S(1)} copy(bf16[1024,10,128]{0,2,1:T(8,128)(2,1)} %bitcast.100) | data formatting | bytes 5242880 | tf_op jit(solution)/shard_map/reshape | solution.py:51
  31.7 1.7 gather_fusion.3
  33.4 3.6 %broadcast_select_fusion = (bf16[4,1024,128]{2,1,0:T(8,128)(2,1)}, bf16[4,1024,128]{2,1,0:T(8,128)(2,1)S(1)}, bf16[4,1024,128]{2,1,0:T(8,128)(2,1)}) fusion(bf16[4,1024,128]{2,1,0:T(8,128)(2,1)} %gather_fusion.3, pred[4]{0:T(512)(128)(4,1)S(1)} %get-tuple-element.11, bf16[4,1024,128]{2,1,0:T(8,128)(2,1)} %gather_fusion.2, bf16[4,1024,128]{2,1,0:T(8,128)(2,1)} %gather_fusion.1), kind=kLoop, calls=%fused_computation.39 | loop fusion | flops 1572864 | bytes 6291460 | tf_op jit(solution)/shard_map/jit(_take)/select_n | solution.py:53
  36.9 1.6 copy.40
  38.5 13.3 %all-to-all-start.2 = ((bf16[1,64,4,4,4,128]{5,3,2,4,0,1:T(4,128)(2,1)}), bf16[1,64,4,4,4,128]{5,3,2,4,0,1:T(4,128)(2,1)}, u32[]{:S(2)}, u32[]{:S(2)}) async-start(bf16[1,64,4,4,4,128]{5,3,2,4,0,1:T(4,128)(2,1)} %copy.40), calls=%async_computation.2 | async-start | bytes 2097152 | tf_op jit(solution)/shard_map/all_to_all | solution.py:60
  51.9 2.8 copy.45
  54.7 25.1 %all-to-all-done.2 = bf16[1,64,4,4,4,128]{5,3,2,4,0,1:T(4,128)(2,1)} async-done(((bf16[1,64,4,4,4,128]{5,3,2,4,0,1:T(4,128)(2,1)}), bf16[1,64,4,4,4,128]{5,3,2,4,0,1:T(4,128)(2,1)}, u32[]{:S(2)}, u32[]{:S(2)}) %all-to-all-start.2) | async-done | bytes 1048608 | tf_op jit(solution)/shard_map/all_to_all | solution.py:60
  79.8 6.7 %all-to-all-start.4 = ((bf16[1,64,4,4,4,128]{5,3,2,4,0,1:T(4,128)(2,1)}), bf16[1,64,4,4,4,128]{5,3,2,4,0,1:T(4,128)(2,1)}, u32[]{:S(2)}, u32[]{:S(2)}) async-start(bf16[1,64,4,4,4,128]{5,3,2,4,0,1:T(4,128)(2,1)} %copy.45), calls=%async_computation.4 | async-start | bytes 2097152 | tf_op jit(solution)/shard_map/all_to_all | solution.py:60
  86.4 2.8 copy.35
  89.2 25.1 %all-to-all-done.4 = bf16[1,64,4,4,4,128]{5,3,2,4,0,1:T(4,128)(2,1)} async-done(((bf16[1,64,4,4,4,128]{5,3,2,4,0,1:T(4,128)(2,1)}), bf16[1,64,4,4,4,128]{5,3,2,4,0,1:T(4,128)(2,1)}, u32[]{:S(2)}, u32[]{:S(2)}) %all-to-all-start.4) | async-done | bytes 1048608 | tf_op jit(solution)/shard_map/all_to_all | solution.py:60
  114.3 6.7 %all-to-all-start = ((bf16[1,64,4,4,4,128]{5,3,2,4,0,1:T(4,128)(2,1)}), bf16[1,64,4,4,4,128]{5,3,2,4,0,1:T(4,128)(2,1)}, u32[]{:S(2)}, u32[]{:S(2)}) async-start(bf16[1,64,4,4,4,128]{5,3,2,4,0,1:T(4,128)(2,1)} %copy.35), calls=%async_computation | async-start | bytes 2097152 | tf_op jit(solution)/shard_map/all_to_all | solution.py:60
  121.0 2.7 copy.41
  123.7 25.2 %all-to-all-done = bf16[1,64,4,4,4,128]{5,3,2,4,0,1:T(4,128)(2,1)} async-done(((bf16[1,64,4,4,4,128]{5,3,2,4,0,1:T(4,128)(2,1)}), bf16[1,64,4,4,4,128]{5,3,2,4,0,1:T(4,128)(2,1)}, u32[]{:S(2)}, u32[]{:S(2)}) %all-to-all-start) | async-done | bytes 1048608 | tf_op jit(solution)/shard_map/all_to_all | solution.py:60
  148.9 4.2 %all-to-all-start.3 = ((bf16[64,1,4,4,4,128]{5,3,0,4,1,2:T(4,128)(2,1)}), bf16[64,1,4,4,4,128]{5,3,0,4,1,2:T(4,128)(2,1)}, u32[]{:S(2)}, u32[]{:S(2)}) async-start(bf16[64,1,4,4,4,128]{5,3,0,4,1,2:T(4,128)(2,1)} %copy.41), calls=%async_computation.3 | async-start | bytes 2097152 | tf_op jit(solution)/shard_map/all_to_all | solution.py:59
  153.2 2.7 copy.46
  155.8 11.1 %all-to-all-done.3 = bf16[64,1,4,4,4,128]{5,3,0,4,1,2:T(4,128)(2,1)} async-done(((bf16[64,1,4,4,4,128]{5,3,0,4,1,2:T(4,128)(2,1)}), bf16[64,1,4,4,4,128]{5,3,0,4,1,2:T(4,128)(2,1)}, u32[]{:S(2)}, u32[]{:S(2)}) %all-to-all-start.3) | async-done | bytes 1048608 | tf_op jit(solution)/shard_map/all_to_all | solution.py:59
  166.9 4.3 %all-to-all-start.5 = ((bf16[64,1,4,4,4,128]{5,3,0,4,1,2:T(4,128)(2,1)}), bf16[64,1,4,4,4,128]{5,3,0,4,1,2:T(4,128)(2,1)}, u32[]{:S(2)}, u32[]{:S(2)}) async-start(bf16[64,1,4,4,4,128]{5,3,0,4,1,2:T(4,128)(2,1)} %copy.46), calls=%async_computation.5 | async-start | bytes 2097152 | tf_op jit(solution)/shard_map/all_to_all | solution.py:59
  171.3 2.7 copy.36
  174.0 9.8 %all-to-all-done.5 = bf16[64,1,4,4,4,128]{5,3,0,4,1,2:T(4,128)(2,1)} async-done(((bf16[64,1,4,4,4,128]{5,3,0,4,1,2:T(4,128)(2,1)}), bf16[64,1,4,4,4,128]{5,3,0,4,1,2:T(4,128)(2,1)}, u32[]{:S(2)}, u32[]{:S(2)}) %all-to-all-start.5) | async-done | bytes 1048608 | tf_op jit(solution)/shard_map/all_to_all | solution.py:59
  183.7 4.4 %all-to-all-start.1 = ((bf16[64,1,4,4,4,128]{5,3,0,4,1,2:T(4,128)(2,1)}), bf16[64,1,4,4,4,128]{5,3,0,4,1,2:T(4,128)(2,1)}, u32[]{:S(2)}, u32[]{:S(2)}) async-start(bf16[64,1,4,4,4,128]{5,3,0,4,1,2:T(4,128)(2,1)} %copy.36), calls=%async_computation.1 | async-start | bytes 2097152 | tf_op jit(solution)/shard_map/all_to_all | solution.py:59
  188.2 3.8 %gather_fusion.4 = bf16[6,1024,128]{2,1,0:T(8,128)(2,1)} fusion(bf16[1024,10,128]{2,0,1:T(8,128)(2,1)} %copy-done, s32[1024]{0:T(1024)S(1)} %pad_clamp_fusion.1), kind=kCustom, calls=%fused_computation.1.clone | custom fusion | bytes 3145752 | tf_op jit(solution)/shard_map/jit(_take)/gather | solution.py:52
  192.0 3.7 %gather_fusion.5 = bf16[6,1024,128]{2,1,0:T(8,128)(2,1)} fusion(bf16[1024,10,128]{2,0,1:T(8,128)(2,1)} %copy.39, s32[1024]{0:T(1024)S(1)} %pad_clamp_fusion.1), kind=kCustom, calls=%fused_computation.4.clone | custom fusion | bytes 3145752 | tf_op jit(solution)/shard_map/jit(_take)/gather | solution.py:52
  196.0 2.5 copy.42
  198.5 2.5 copy.47
  201.1 1.6 copy.37
  204.7 1.6 divide_convert_fusion.1
  206.3 1.8 copy.64
  208.2 11.8 %all-to-all-start.6 = ((bf16[64,1,1,4,16,128]{5,3,4,2,1,0:T(4,128)(2,1)}), bf16[64,1,1,4,16,128]{5,3,4,2,1,0:T(4,128)(2,1)}, u32[]{:S(2)}, u32[]{:S(2)}) async-start(bf16[64,1,1,4,16,128]{5,3,4,2,1,0:T(4,128)(2,1)} %bitcast.111), calls=%async_computation.6 | async-start | bytes 2097152 | tf_op jit(solution)/shard_map/all_to_all | solution.py:80
  220.2 1.0 copy-done.1
  221.2 12.4 %fusion = (f32[6,1024]{1,0:T(8,128)S(1)}, f32[6,1024,1024]{1,2,0:T(8,128)}) fusion(pred[1024,1024]{0,1:T(8,128)(4,1)S(1)} %bitcast.102, bf16[6,1024,128]{2,1,0:T(8,128)(2,1)} %gather_fusion.5, pred[6]{0:T(512)(128)(4,1)S(1)} %get-tuple-element.13, bf16[6,1024,128]{2,1,0:T(8,128)(2,1)} %gather_fusion.4), kind=kOutput, calls=%fused_computation.9 | convolution fusion | flops 1631053824 | bytes 29384710 | tf_op jit(solution)/shard_map/bqhd,bkhd->bhqk/dot_general | solution.py:24
  233.7 1.9 gather_fusion.6
  235.6 11.5 %fusion.1 = f32[6,1024]{1,0:T(8,128)S(1)} fusion(f32[6,1024,1024]{1,2,0:T(8,128)} %get-tuple-element.19, f32[6,1024]{1,0:T(8,128)S(1)} %get-tuple-element.18, pred[1024,1024]{0,1:T(8,128)(4,1)} %bitcast.103), kind=kLoop, calls=%fused_computation.10 | loop fusion | flops 25159680 | bytes 26263552 | tf_op jit(solution)/shard_map/reduce_sum | solution.py:29
  247.8 2.9 %copy.50 = bf16[1,64,1,4,16,128]{5,1,3,2,0,4:T(8,128)(2,1)} copy(bf16[1,64,1,4,16,128]{5,3,4,1,2,0:T(4,128)(2,1)} %bitcast.35) | data formatting | bytes 2097152 | tf_op jit(solution)/shard_map/all_to_all | solution.py:80
  250.7 3.7 %all-to-all-start.7 = ((bf16[1,64,1,4,16,128]{5,1,3,2,0,4:T(8,128)(2,1)}), bf16[1,64,1,4,16,128]{5,1,3,2,0,4:T(8,128)(2,1)S(1)}, u32[]{:S(2)}, u32[]{:S(2)}) async-start(bf16[1,64,1,4,16,128]{5,1,3,2,0,4:T(8,128)(2,1)} %copy.50), calls=%async_computation.7 | async-start | bytes 2097152 | tf_op jit(solution)/shard_map/all_to_all | solution.py:79
  254.5 13.6 %fusion.22 = bf16[1024,6,128]{2,0,1:T(8,128)(2,1)} fusion(f32[6,1024]{1,0:T(8,128)S(1)} %fusion.1, bf16[6,1024,128]{2,1,0:T(8,128)(2,1)} %gather_fusion.6, pred[6]{0:T(512)(128)(4,1)S(1)} %get-tuple-element.13, f32[6,1024,1024]{1,2,0:T(8,128)} %get-tuple-element.19, f32[6,1024]{1,0:T(8,128)S(1)} %get-tuple-element.18, pred[1024,1024]{0,1:T(8,128)(4,1)S(1)} %bitcast.104), kind=kOutput, calls=%fused_computation.35 | convolution fusion | flops 1638137856 | bytes 29409286 | tf_op jit(solution)/shard_map/bhqk,bkhd->bhqd/dot_general | solution.py:31
  268.1 1.3 sort.35
  271.1 2.5 gather_fusion
  273.6 3.0 %copy.56 = bf16[1024,10,128]{0,2,1:T(8,128)(2,1)S(1)} copy(bf16[1024,10,128]{2,0,1:T(8,128)(2,1)} %bitcast.97) | data formatting | bytes 5242880 | tf_op jit(solution)/shard_map/jit(_take)/gather | solution.py:91
  276.6 2.0 bitcast_select_fusion
  278.6 4.4 %copy.57 = bf16[1024,1280]{1,0:T(8,128)(2,1)} copy(bf16[1024,1280]{0,1:T(8,128)(2,1)} %bitcast_select_fusion) | data formatting | bytes 5242880 | tf_op jit(solution)/shard_map/jit(_take)/select_n | solution.py:91
  (41 shorter events, 5.9 us)
Async XLA Ops:
  9.6 9.4 %copy-start = (bf16[1024,10,128]{2,0,1:T(8,128)(2,1)}, bf16[1024,10,128]{2,0,1:T(8,128)(2,1)S(1)}, u32[]{:S(2)}) copy-start(bf16[1024,10,128]{2,0,1:T(8,128)(2,1)S(1)} %copy.34) | copy-start | bytes 7864324
  38.5 41.3 %all-to-all-start.2 = ((bf16[1,64,4,4,4,128]{5,3,2,4,0,1:T(4,128)(2,1)}), bf16[1,64,4,4,4,128]{5,3,2,4,0,1:T(4,128)(2,1)}, u32[]{:S(2)}, u32[]{:S(2)}) async-start(bf16[1,64,4,4,4,128]{5,3,2,4,0,1:T(4,128)(2,1)} %copy.40), calls=%async_computation.2 | async-start | bytes 2097152 | tf_op jit(solution)/shard_map/all_to_all | solution.py:60
  79.8 34.6 %all-to-all-start.4 = ((bf16[1,64,4,4,4,128]{5,3,2,4,0,1:T(4,128)(2,1)}), bf16[1,64,4,4,4,128]{5,3,2,4,0,1:T(4,128)(2,1)}, u32[]{:S(2)}, u32[]{:S(2)}) async-start(bf16[1,64,4,4,4,128]{5,3,2,4,0,1:T(4,128)(2,1)} %copy.45), calls=%async_computation.4 | async-start | bytes 2097152 | tf_op jit(solution)/shard_map/all_to_all | solution.py:60
  114.3 34.6 %all-to-all-start = ((bf16[1,64,4,4,4,128]{5,3,2,4,0,1:T(4,128)(2,1)}), bf16[1,64,4,4,4,128]{5,3,2,4,0,1:T(4,128)(2,1)}, u32[]{:S(2)}, u32[]{:S(2)}) async-start(bf16[1,64,4,4,4,128]{5,3,2,4,0,1:T(4,128)(2,1)} %copy.35), calls=%async_computation | async-start | bytes 2097152 | tf_op jit(solution)/shard_map/all_to_all | solution.py:60
  148.9 18.0 %all-to-all-start.3 = ((bf16[64,1,4,4,4,128]{5,3,0,4,1,2:T(4,128)(2,1)}), bf16[64,1,4,4,4,128]{5,3,0,4,1,2:T(4,128)(2,1)}, u32[]{:S(2)}, u32[]{:S(2)}) async-start(bf16[64,1,4,4,4,128]{5,3,0,4,1,2:T(4,128)(2,1)} %copy.41), calls=%async_computation.3 | async-start | bytes 2097152 | tf_op jit(solution)/shard_map/all_to_all | solution.py:59
  166.9 16.8 %all-to-all-start.5 = ((bf16[64,1,4,4,4,128]{5,3,0,4,1,2:T(4,128)(2,1)}), bf16[64,1,4,4,4,128]{5,3,0,4,1,2:T(4,128)(2,1)}, u32[]{:S(2)}, u32[]{:S(2)}) async-start(bf16[64,1,4,4,4,128]{5,3,0,4,1,2:T(4,128)(2,1)} %copy.46), calls=%async_computation.5 | async-start | bytes 2097152 | tf_op jit(solution)/shard_map/all_to_all | solution.py:59
  183.7 17.4 %all-to-all-start.1 = ((bf16[64,1,4,4,4,128]{5,3,0,4,1,2:T(4,128)(2,1)}), bf16[64,1,4,4,4,128]{5,3,0,4,1,2:T(4,128)(2,1)}, u32[]{:S(2)}, u32[]{:S(2)}) async-start(bf16[64,1,4,4,4,128]{5,3,0,4,1,2:T(4,128)(2,1)} %copy.36), calls=%async_computation.1 | async-start | bytes 2097152 | tf_op jit(solution)/shard_map/all_to_all | solution.py:59
  192.0 3.7 %copy-start.7 = (s32[4,2,2]{0,2,1:T(2,128)S(1)}, s32[4,2,2]{0,2,1:T(2,128)}, u32[]{:S(2)}) copy-start(s32[4,2,2]{0,2,1:T(2,128)} %param.15) | copy-start | bytes 196
  192.0 4.0 %copy-start.6 = (s32[1,8,8]{2,1,0:T(8,128)S(1)}, s32[1,8,8]{2,1,0:T(8,128)}, u32[]{:S(2)}) copy-start(s32[1,8,8]{2,1,0:T(8,128)} %param.14) | copy-start | bytes 772
  201.1 1.6 copy-start.3
  203.5 1.2 copy-start.5
  208.2 39.7 %all-to-all-start.6 = ((bf16[64,1,1,4,16,128]{5,3,4,2,1,0:T(4,128)(2,1)}), bf16[64,1,1,4,16,128]{5,3,4,2,1,0:T(4,128)(2,1)}, u32[]{:S(2)}, u32[]{:S(2)}) async-start(bf16[64,1,1,4,16,128]{5,3,4,2,1,0:T(4,128)(2,1)} %bitcast.111), calls=%async_computation.6 | async-start | bytes 2097152 | tf_op jit(solution)/shard_map/all_to_all | solution.py:80
  220.2 1.0 copy-start.1
  247.1 7.4 %copy-start.2 = (pred[1024,8,128]{0,2,1:T(8,128)(4,1)S(1)}, pred[1024,8,128]{0,2,1:T(8,128)(4,1)}, u32[]{:S(2)}) copy-start(pred[1024,8,128]{0,2,1:T(8,128)(4,1)} %copy-done.1) | copy-start | bytes 3145732
  250.7 18.7 %all-to-all-start.7 = ((bf16[1,64,1,4,16,128]{5,1,3,2,0,4:T(8,128)(2,1)}), bf16[1,64,1,4,16,128]{5,1,3,2,0,4:T(8,128)(2,1)S(1)}, u32[]{:S(2)}, u32[]{:S(2)}) async-start(bf16[1,64,1,4,16,128]{5,1,3,2,0,4:T(8,128)(2,1)} %copy.50), calls=%async_computation.7 | async-start | bytes 2097152 | tf_op jit(solution)/shard_map/all_to_all | solution.py:79
  269.4 1.4 copy-start.4
where the time goes:
time: 285 us; the launch traced here: 283 us
  waiting for transfers between devices  97 us (34%)
  local copies, waits for them, and re-layouts  80.6 us (28%)
  starting transfers between devices  55.1 us (19%)
  matrix products  28.4 us (10%)
  other arithmetic  21.5 us (8%)
    all_to_all x3, waiting for transfers between devices, on_device(): lax.all_to_all(shortened(parts), 'seq', split_axis=1, concat_axis=0, tile...  75.4 us
    all_to_all x3, starting transfers between devices, on_device(): lax.all_to_all(shortened(parts), 'seq', split_axis=1, concat_axis=0, tile...  26.7 us
    all_to_all x3, waiting for transfers between devices, on_device(): lax.all_to_all(lax.all_to_all(shortened(parts), 'seq', split_axis=1, conc...  20.8 us
    unnamed x21, local copies, waits for them, and re-layouts  15.7 us
    dot_general x2, matrix products, attend(): jnp.einsum('bhqk,bkhd->bhqd', weights.astype(jnp.bfloat16), value_rows, p...  15.2 us
    dot_general x2, matrix products, attend(): jnp.einsum('bqhd,bkhd->bhqk', query, key_rows, preferred_element_type=jnp...  13.2 us
    all_to_all x3, starting transfers between devices, on_device(): lax.all_to_all(lax.all_to_all(shortened(parts), 'seq', split_axis=1, conc...  13 us
    reduce_sum x2, other arithmetic, attend(): total = jnp.sum(weights, axis=-1, keepdims=True)  12.4 us
  transfers between devices with their start and end apart: 8, of which 6 were waited for; matrix products, arithmetic and copies ran while one was open for 24% of the time, Pallas kernels for 0%

commit v1 on v0

v1 whole, which is shorter than its diff:
```python
import functools
import math

import jax
import jax.numpy as jnp
from jax import lax
from jax.experimental import pallas as pl
from jax.experimental.pallas import tpu as pltpu
from jax.sharding import PartitionSpec as P

HEAD_DIM = 128
TILE = 128
LOCAL_HEADS = 10
HT_DEV = 4
HS_DEV = LOCAL_HEADS - HT_DEV
ROWS = 1024
SEQ = 64
PIECE = ROWS // SEQ
NZ, NY, NC = 8, 4, 2
STEP = 256
EXP_SCALE = HEAD_DIM**-0.5 * math.log2(math.e)
NEG = -1e30
MESH = pl.DeviceIdType.MESH


def attend_rows(query, key_rows, value_rows, bias):
    scores = lax.dot_general(
        query, key_rows, (((1,), (1,)), ((), ())), preferred_element_type=jnp.float32
    )
    lows, totals = [], []
    for a in range(STEP // TILE):
        row = [
            scores[a * TILE : (a + 1) * TILE, b * TILE : (b + 1) * TILE] + bias(a, b)
            for b in range(ROWS // TILE)
        ]
        top = jnp.max(functools.reduce(jnp.maximum, row), axis=1, keepdims=True)
        weights = [jnp.exp2((part - top) * EXP_SCALE) for part in row]
        totals.append(jnp.sum(functools.reduce(jnp.add, weights), axis=1, keepdims=True))
        lows.append(jnp.concatenate([w.astype(jnp.bfloat16) for w in weights], axis=1))
    low = jnp.concatenate(lows, axis=0)
    total = jnp.concatenate(totals, axis=0)
    mixed = jnp.dot(low, value_rows, preferred_element_type=jnp.float32)
    return (mixed / total).astype(jnp.bfloat16)


def main_kernel(
    head_class, mask_s, mask_t, q_hbm, k_hbm, v_hbm, out,
    q_all, k_all, v_all, pack, recv, o_send, s_out, t_bias,
    in_sem, send_sem, recv_sem, o_send_sem, o_recv_sem, s_sem,
):
    me = lax.axis_index("seq")
    head = lax.axis_index("head")
    z, y, c = me // (NY * NC), (me // NC) % NY, me % NC

    def peer(i):
        dz, dy, dc = (i * 3) % NZ, (i // NZ) % NY, i // (NZ * NY)
        return ((z + dz) % NZ) * (NY * NC) + ((y + dy) % NY) * NC + (c + dc) % NC

    for n, (src, dst) in enumerate(((q_hbm, q_all), (k_hbm, k_all), (v_hbm, v_all))):
        for j in range(LOCAL_HEADS):
            cols = pl.ds(j * HEAD_DIM, HEAD_DIM)
            pltpu.make_async_copy(src.at[:, cols], dst.at[j], in_sem.at[n]).start()

    barrier = pltpu.get_barrier_semaphore()

    def greet(i, carry):
        pl.semaphore_signal(barrier, inc=1, device_id=(peer(i), head), device_id_type=MESH)
        return carry

    lax.fori_loop(1, SEQ, greet, 0)

    ranks, count_t, count_s = [], jnp.int32(0), jnp.int32(HT_DEV)
    for j in range(LOCAL_HEADS):
        is_t = head_class[j] > 0
        ranks.append(jnp.where(is_t, count_t, count_s))
        count_t = count_t + jnp.where(is_t, 1, 0)
        count_s = count_s + jnp.where(is_t, 0, 1)

    def head_of(n):
        place = jnp.int32(0)
        for j, rank in enumerate(ranks):
            place = jnp.where(rank == n, j, place)
        return place

    for n, whole in enumerate((q_all, k_all, v_all)):
        pltpu.make_async_copy(whole, whole, in_sem.at[n]).wait()

    def pack_head(t):
        place = head_of(t)
        for n, whole in enumerate((q_all, k_all, v_all)):
            pack[t, :, n] = whole[place].reshape(SEQ, PIECE, HEAD_DIM)

    def send_head(t):
        pltpu.make_async_copy(pack.at[t, me], recv.at[t, me], recv_sem.at[t]).start()

        def send(i, carry):
            other = peer(i)
            pltpu.make_async_remote_copy(
                src_ref=pack.at[t, other],
                dst_ref=recv.at[t, me],
                send_sem=send_sem.at[t],
                recv_sem=recv_sem.at[t],
                device_id=(other, head),
                device_id_type=MESH,
            ).start()
            return carry

        lax.fori_loop(1, SEQ, send, 0)

    pack_head(0)
    pl.semaphore_wait(barrier, SEQ - 1)
    send_head(0)
    for t in range(1, HT_DEV):
        pack_head(t)
        send_head(t)

    row = lax.broadcasted_iota(jnp.int32, (TILE, TILE), 0) % PIECE // 2
    col = lax.broadcasted_iota(jnp.int32, (TILE, TILE), 1) % PIECE // 2
    bias = jnp.full((TILE, TILE), NEG, jnp.float32)
    for g in range(mask_t.shape[0]):
        for i in range(2):
            for j in range(2):
                value = jnp.where(mask_t[g, i, j] > 0, 0.0, NEG).astype(jnp.float32)
                bias = jnp.where((row == 2 * g + i) & (col == 2 * g + j), value, bias)
    t_bias[...] = bias

    def spatial_head(n, carry):
        place = head_of(HT_DEV + n)

        def block(r, inner):
            at = pl.multiple_of(r * STEP, STEP)

            def tile_bias(a, b):
                allowed = mask_s[0, r * (STEP // TILE) + a, b] > 0
                return jnp.where(allowed, 0.0, NEG).astype(jnp.float32)

            s_out[n, pl.ds(at, STEP)] = attend_rows(
                q_all[place, pl.ds(at, STEP)], k_all[place], v_all[place], tile_bias
            )
            return inner

        lax.fori_loop(0, ROWS // STEP, block, 0)
        pltpu.make_async_copy(s_out.at[n], out.at[HT_DEV + n], s_sem.at[n]).start()
        return carry

    lax.fori_loop(0, HS_DEV, spatial_head, 0)

    def temporal_head(t, carry):
        pltpu.make_async_copy(recv.at[t], recv.at[t], recv_sem.at[t]).wait()

        def block(r, inner):
            frames = STEP // PIECE
            at = pl.ds(r * frames, frames)
            mixed = attend_rows(
                recv[t, at, 0].reshape(STEP, HEAD_DIM),
                recv[t, :, 1].reshape(ROWS, HEAD_DIM),
                recv[t, :, 2].reshape(ROWS, HEAD_DIM),
                lambda a, b: t_bias[...],
            )
            o_send[t, at] = mixed.reshape(frames, PIECE, HEAD_DIM)
            return inner

        lax.fori_loop(0, ROWS // STEP, block, 0)
        mine = pl.ds(pl.multiple_of(me * PIECE, PIECE), PIECE)
        pltpu.make_async_copy(o_send.at[t, me], out.at[t, mine], o_recv_sem.at[t]).start()

        def send(i, inner):
            other = peer(i)
            pltpu.make_async_remote_copy(
                src_ref=o_send.at[t, other],
                dst_ref=out.at[t, mine],
                send_sem=o_send_sem.at[t],
                recv_sem=o_recv_sem.at[t],
                device_id=(other, head),
                device_id_type=MESH,
            ).start()
            return inner

        lax.fori_loop(1, SEQ, send, 0)
        return carry

    lax.fori_loop(0, HT_DEV, temporal_head, 0)

    def finish(t, carry):
        sent = pack.at[t, pl.ds(0, SEQ - 1)]
        pltpu.make_async_copy(sent, sent, send_sem.at[t]).wait()
        sent = o_send.at[t, pl.ds(0, SEQ - 1)]
        pltpu.make_async_copy(sent, sent, o_send_sem.at[t]).wait()
        pltpu.make_async_copy(out.at[t], out.at[t], o_recv_sem.at[t]).wait()
        return carry

    def finish_spatial(n, carry):
        pltpu.make_async_copy(s_out.at[n], out.at[HT_DEV + n], s_sem.at[n]).wait()
        return carry

    lax.fori_loop(0, HS_DEV, finish_spatial, 0)
    lax.fori_loop(0, HT_DEV, finish, 0)


def place_kernel(head_class, packed, out, sem):
    count_t, count_s = jnp.int32(0), jnp.int32(HT_DEV)
    copies = []
    for j in range(LOCAL_HEADS):
        is_t = head_class[j] > 0
        rank = jnp.where(is_t, count_t, count_s)
        count_t = count_t + jnp.where(is_t, 1, 0)
        count_s = count_s + jnp.where(is_t, 0, 1)
        copy = pltpu.make_async_copy(
            packed.at[rank], out.at[:, pl.ds(j * HEAD_DIM, HEAD_DIM)], sem.at[j]
        )
        copy.start()
        copies.append(copy)
    for copy in copies:
        copy.wait()


def on_device(queries, keys, values, head_class, mask_spatial, mask_temporal):
    smem = pl.BlockSpec(memory_space=pltpu.SMEM)
    anywhere = pl.BlockSpec(memory_space=pl.ANY)
    whole = pltpu.VMEM((LOCAL_HEADS, ROWS, HEAD_DIM), jnp.bfloat16)
    moved = pltpu.VMEM((HT_DEV, SEQ, 3, PIECE, HEAD_DIM), jnp.bfloat16)
    packed = pl.pallas_call(
        main_kernel,
        out_shape=jax.ShapeDtypeStruct((LOCAL_HEADS, ROWS, HEAD_DIM), jnp.bfloat16),
        in_specs=[smem] * 3 + [anywhere] * 3,
        out_specs=anywhere,
        scratch_shapes=[
            whole, whole, whole, moved, moved,
            pltpu.VMEM((HT_DEV, SEQ, PIECE, HEAD_DIM), jnp.bfloat16),
            pltpu.VMEM((HS_DEV, ROWS, HEAD_DIM), jnp.bfloat16),
            pltpu.VMEM((TILE, TILE), jnp.float32),
            pltpu.SemaphoreType.DMA((3,)),
            pltpu.SemaphoreType.DMA((HT_DEV,)),
            pltpu.SemaphoreType.DMA((HT_DEV,)),
            pltpu.SemaphoreType.DMA((HT_DEV,)),
            pltpu.SemaphoreType.DMA((HT_DEV,)),
            pltpu.SemaphoreType.DMA((HS_DEV,)),
        ],
        compiler_params=pltpu.CompilerParams(
            collective_id=0, has_side_effects=True, vmem_limit_bytes=56 << 20
        ),
        cost_estimate=pl.CostEstimate(
            flops=10 * 4 * ROWS * ROWS * HEAD_DIM,
            bytes_accessed=10 << 20,
            transcendentals=10 * ROWS * ROWS,
        ),
        name="attend_and_move",
    )(head_class, mask_spatial, mask_temporal, queries, keys, values)
    return pl.pallas_call(
        place_kernel,
        out_shape=jax.ShapeDtypeStruct((ROWS, LOCAL_HEADS * HEAD_DIM), jnp.bfloat16),
        in_specs=[smem, anywhere],
        out_specs=anywhere,
        scratch_shapes=[pltpu.SemaphoreType.DMA((LOCAL_HEADS,))],
        name="place_heads",
    )(head_class, packed)


def solution(mesh):
    return jax.shard_map(
        on_device,
        mesh=mesh,
        in_specs=(
            P("seq", "head"),
            P("seq", "head"),
            P("seq", "head"),
            P("head"),
            P("seq", None, None),
            P("seq", None, None),
        ),
        out_specs=P("seq", "head"),
        check_vma=False,
    )
```

time: 285 us -> 190 us (0.67)
  Pallas kernels: 0 us -> 188 us
  waiting for transfers between devices: 97 us -> 0 us
  local copies, waits for them, and re-layouts: 80.6 us -> 1.36 us
  starting transfers between devices: 55.1 us -> 0 us
  matrix products: 28.4 us -> 0 us
  other arithmetic: 21.5 us -> 0 us
    pallas_call x0 -> x2, Pallas kernels: none -> 188 us  [the longest x1 107 us: on_device(): pl.pallas_call(main_kernel, out_shape=jax.ShapeDtypeStruct((LOCAL_HEADS,...]
    all_to_all x8 -> x0, waiting for transfers between devices: 97 us -> none  [the longest x3 75.4 us: on_device(): lax.all_to_all(shortened(parts), 'seq', split_axis=1, concat_axis=0, tile...]
    all_to_all x8 -> x0, starting transfers between devices: 55.1 us -> none  [the longest x3 26.7 us: on_device(): lax.all_to_all(shortened(parts), 'seq', split_axis=1, concat_axis=0, tile...]
    dot_general x4 -> x0, matrix products: 28.4 us -> none  [the longest x2 15.2 us: attend(): jnp.einsum('bhqk,bkhd->bhqd', weights.astype(jnp.bfloat16), value_rows, p...]
    reshape x10 -> x0, local copies, waits for them, and re-layouts: 26.4 us -> none  [the longest x3 10.9 us: on_device(): a.reshape(rows, local_heads, HEAD_DIM)]
    gather x8 -> x0, local copies, waits for them, and re-layouts: 21.7 us -> none  [the longest x3 9.42 us: on_device(): spatial = [jnp.take(a, chosen_s, axis=1) for a in shaped]]
    unnamed x21 -> x1, local copies, waits for them, and re-layouts: 15.7 us -> 1.36 us
    reduce_sum x2 -> x0, other arithmetic: 12.4 us -> none  [attend(): total = jnp.sum(weights, axis=-1, keepdims=True)]
  transfers between devices with their start and end apart: 8 -> 0, of which waited for: 6 -> 0; matrix products, arithmetic and copies ran while one was open for 24% -> 0% of each run, Pallas kernels for 0% -> 0%
where the time goes in v1:
time: 190 us; the launch traced here: 189 us
  Pallas kernels  188 us (99%)
    pallas_call x1, Pallas kernels, on_device(): pl.pallas_call(main_kernel, out_shape=jax.ShapeDtypeStruct((LOCAL_HEADS,...  107 us
    pallas_call x1, Pallas kernels, on_device(): pl.pallas_call(place_kernel, out_shape=jax.ShapeDtypeStruct((ROWS, LOCAL_...  81.3 us

profile of v1, /device:TPU:1, one launch (start us, length us, event | category | flops | bytes accessed | tf_op | source)
XLA Modules:
  0.0 189.5 jit_solution(9475836968758842889)
XLA Ops:
  0.0 1.4 copy.7.mask_t
  1.4 106.9 %attend_and_move.1.packed = bf16[10,1024,128]{2,1,0:T(8,128)(2,1)} custom-call(s32[10]{0:T(128)} %head_class.3, s32[1,8,8]{2,1,0:T(8,128)} %mask_s.1, s32[4,2,2]{2,1,0:T(2,128)} %copy.7.mask_t, bf16[1024,1280]{1,0:T(8,128)(2,1)} %q_hbm.1, bf16[1024,1280]{1,0:T(8,128)(2,1)} %k_hbm.1, bf16[1024,1280]{1,0:T(8,128)(2,1)} %v_hbm.1), custom_call_target="tpu_custom_call" | custom-call | flops 5368709120 | bytes 10485760 | tf_op jit(solution)/shard_map/attend_and_move/pallas_call | solution.py:222
  108.2 81.3 %place_heads.1 = bf16[1024,1280]{1,0:T(8,128)(2,1)} custom-call(s32[10]{0:T(128)} %head_class.3, bf16[10,1024,128]{2,1,0:T(8,128)(2,1)} %attend_and_move.1.packed), custom_call_target="tpu_custom_call" | custom-call | tf_op jit(solution)/shard_map/place_heads/pallas_call | solution.py:249

commit v2 on v1

--- a/solution.py
+++ b/solution.py
@@ -45,8 +45,8 @@
 
 def main_kernel(
     head_class, mask_s, mask_t, q_hbm, k_hbm, v_hbm, out,
-    q_all, k_all, v_all, pack, recv, o_send, s_out, t_bias,
-    in_sem, send_sem, recv_sem, o_send_sem, o_recv_sem, s_sem,
+    q_all, k_all, v_all, pack, recv, o_send, t_bias,
+    in_sem, send_sem, recv_sem, o_send_sem, o_recv_sem,
 ):
     me = lax.axis_index("seq")
     head = lax.axis_index("head")
@@ -117,10 +117,10 @@
     row = lax.broadcasted_iota(jnp.int32, (TILE, TILE), 0) % PIECE // 2
     col = lax.broadcasted_iota(jnp.int32, (TILE, TILE), 1) % PIECE // 2
     bias = jnp.full((TILE, TILE), NEG, jnp.float32)
-    for g in range(mask_t.shape[0]):
+    for g in range(mask_t.shape[2]):
         for i in range(2):
             for j in range(2):
-                value = jnp.where(mask_t[g, i, j] > 0, 0.0, NEG).astype(jnp.float32)
+                value = jnp.where(mask_t[i, j, g] > 0, 0.0, NEG).astype(jnp.float32)
                 bias = jnp.where((row == 2 * g + i) & (col == 2 * g + j), value, bias)
     t_bias[...] = bias
 
@@ -134,13 +134,12 @@
                 allowed = mask_s[0, r * (STEP // TILE) + a, b] > 0
                 return jnp.where(allowed, 0.0, NEG).astype(jnp.float32)
 
-            s_out[n, pl.ds(at, STEP)] = attend_rows(
+            out[HT_DEV + n, pl.ds(at, STEP)] = attend_rows(
                 q_all[place, pl.ds(at, STEP)], k_all[place], v_all[place], tile_bias
             )
             return inner
 
         lax.fori_loop(0, ROWS // STEP, block, 0)
-        pltpu.make_async_copy(s_out.at[n], out.at[HT_DEV + n], s_sem.at[n]).start()
         return carry
 
     lax.fori_loop(0, HS_DEV, spatial_head, 0)
@@ -189,11 +188,6 @@
         pltpu.make_async_copy(out.at[t], out.at[t], o_recv_sem.at[t]).wait()
         return carry
 
-    def finish_spatial(n, carry):
-        pltpu.make_async_copy(s_out.at[n], out.at[HT_DEV + n], s_sem.at[n]).wait()
-        return carry
-
-    lax.fori_loop(0, HS_DEV, finish_spatial, 0)
     lax.fori_loop(0, HT_DEV, finish, 0)
 
 
@@ -221,23 +215,21 @@
     moved = pltpu.VMEM((HT_DEV, SEQ, 3, PIECE, HEAD_DIM), jnp.bfloat16)
     packed = pl.pallas_call(
         main_kernel,
-        out_shape=jax.ShapeDtypeStruct((LOCAL_HEADS, ROWS, HEAD_DIM), jnp.bfloat16),
+        out_shape=pltpu.VMEM((LOCAL_HEADS, ROWS, HEAD_DIM), jnp.bfloat16),
         in_specs=[smem] * 3 + [anywhere] * 3,
-        out_specs=anywhere,
+        out_specs=pl.BlockSpec(memory_space=pltpu.VMEM),
         scratch_shapes=[
             whole, whole, whole, moved, moved,
             pltpu.VMEM((HT_DEV, SEQ, PIECE, HEAD_DIM), jnp.bfloat16),
-            pltpu.VMEM((HS_DEV, ROWS, HEAD_DIM), jnp.bfloat16),
             pltpu.VMEM((TILE, TILE), jnp.float32),
             pltpu.SemaphoreType.DMA((3,)),
             pltpu.SemaphoreType.DMA((HT_DEV,)),
             pltpu.SemaphoreType.DMA((HT_DEV,)),
             pltpu.SemaphoreType.DMA((HT_DEV,)),
             pltpu.SemaphoreType.DMA((HT_DEV,)),
-            pltpu.SemaphoreType.DMA((HS_DEV,)),
         ],
         compiler_params=pltpu.CompilerParams(
-            collective_id=0, has_side_effects=True, vmem_limit_bytes=56 << 20
+            collective_id=0, has_side_effects=True, vmem_limit_bytes=60 << 20
         ),
         cost_estimate=pl.CostEstimate(
             flops=10 * 4 * ROWS * ROWS * HEAD_DIM,
@@ -245,7 +237,7 @@
             transcendentals=10 * ROWS * ROWS,
         ),
         name="attend_and_move",
-    )(head_class, mask_spatial, mask_temporal, queries, keys, values)
+    )(head_class, mask_spatial, jnp.transpose(mask_temporal, (1, 2, 0)), queries, keys, values)
     return pl.pallas_call(
         place_kernel,
         out_shape=jax.ShapeDtypeStruct((ROWS, LOCAL_HEADS * HEAD_DIM), jnp.bfloat16),

time: 190 us -> 190 us (level)
  no operation moved by 1% of the time
where the time goes in v2:
time: 190 us; the launch traced here: 189 us
  Pallas kernels  188 us (99%)
    pallas_call x1, Pallas kernels, on_device(): pl.pallas_call(main_kernel, out_shape=pltpu.VMEM((LOCAL_HEADS, ROWS, HEAD...  107 us
    pallas_call x1, Pallas kernels, on_device(): pl.pallas_call(place_kernel, out_shape=jax.ShapeDtypeStruct((ROWS, LOCAL_...  81.3 us

profile of v2, /device:TPU:1, one launch (start us, length us, event | category | flops | bytes accessed | tf_op | source)
XLA Modules:
  0.0 189.5 jit_solution(5923144395892431570)
XLA Ops:
  0.0 106.7 %attend_and_move.1.packed = bf16[10,1024,128]{2,1,0:T(8,128)(2,1)S(1)} custom-call(s32[10]{0:T(128)} %head_class.3, s32[1,8,8]{2,1,0:T(8,128)} %mask_s.1, s32[2,2,4]{2,1,0:T(2,128)} %bitcast.1, bf16[1024,1280]{1,0:T(8,128)(2,1)} %q_hbm.1, bf16[1024,1280]{1,0:T(8,128)(2,1)} %k_hbm.1, bf16[1024,1280]{1,0:T(8,128)(2,1)} %v_hbm.1), custom_call_target="tpu_custom_call" | custom-call | flops 5368709120 | bytes 10485760 | tf_op jit(solution)/shard_map/attend_and_move/pallas_call | solution.py:216
  106.7 0.0 copy-start
  106.7 1.5 copy-done
  108.2 81.3 %place_heads.1 = bf16[1024,1280]{1,0:T(8,128)(2,1)} custom-call(s32[10]{0:T(128)} %head_class.3, bf16[10,1024,128]{2,1,0:T(8,128)(2,1)} %copy-done), custom_call_target="tpu_custom_call" | custom-call | tf_op jit(solution)/shard_map/place_heads/pallas_call | solution.py:241
Async XLA Ops:
  106.7 1.5 copy-start

commit v3 on v2

--- a/solution.py
+++ b/solution.py
@@ -244,8 +244,9 @@
         in_specs=[smem, anywhere],
         out_specs=anywhere,
         scratch_shapes=[pltpu.SemaphoreType.DMA((LOCAL_HEADS,))],
+        compiler_params=pltpu.CompilerParams(vmem_limit_bytes=8 << 20),
         name="place_heads",
-    )(head_class, packed)
+    )(head_class, pltpu.with_memory_space_constraint(packed, pltpu.VMEM))
 
 
 def solution(mesh):

time: 190 us -> 109 us (0.57)
  Pallas kernels: 188 us -> 109 us
    pallas_call x1, Pallas kernels: 81.3 us -> 2.11 us  [on_device(): pl.pallas_call(place_kernel, out_shape=jax.ShapeDtypeStruct((ROWS, LOCAL_...]
where the time goes in v3:
time: 109 us
  Pallas kernels  109 us (100%)
    pallas_call x1, Pallas kernels, on_device(): pl.pallas_call(main_kernel, out_shape=pltpu.VMEM((LOCAL_HEADS, ROWS, HEAD...  107 us

profile of v3, /device:TPU:1, one launch (start us, length us, event | category | flops | bytes accessed | tf_op | source)
XLA Modules:
  0.0 108.9 jit_solution(15906428038779297132)
XLA Ops:
  0.0 0.0 copy-start
  0.0 106.8 %attend_and_move.1.packed = bf16[10,1024,128]{2,1,0:T(8,128)(2,1)S(1)} custom-call(s32[10]{0:T(128)} %head_class.3, s32[1,8,8]{2,1,0:T(8,128)} %mask_s.1, s32[2,2,4]{2,1,0:T(2,128)} %bitcast.1, bf16[1024,1280]{1,0:T(8,128)(2,1)} %q_hbm.1, bf16[1024,1280]{1,0:T(8,128)(2,1)} %k_hbm.1, bf16[1024,1280]{1,0:T(8,128)(2,1)} %v_hbm.1), custom_call_target="tpu_custom_call" | custom-call | flops 5368709120 | bytes 10485760 | tf_op jit(solution)/shard_map/attend_and_move/pallas_call | solution.py:216
  106.8 0.0 copy-done
  106.8 2.1 %place_heads.1 = bf16[1024,1280]{1,0:T(8,128)(2,1)} custom-call(s32[10]{0:T(128)S(1)} %copy-done, bf16[10,1024,128]{2,1,0:T(8,128)(2,1)S(1)} %attend_and_move.1.packed), custom_call_target="tpu_custom_call" | custom-call | tf_op jit(solution)/shard_map/place_heads/pallas_call | solution.py:241
Async XLA Ops:
  0.0 106.8 %copy-start = (s32[10]{0:T(128)S(1)}, s32[10]{0:T(128)}, u32[]{:S(2)}) copy-start(s32[10]{0:T(128)} %head_class.3) | copy-start | bytes 124

commit v4 on v3

--- a/solution.py
+++ b/solution.py
@@ -45,29 +45,67 @@
 
 def main_kernel(
     head_class, mask_s, mask_t, q_hbm, k_hbm, v_hbm, out,
-    q_all, k_all, v_all, pack, recv, o_send, t_bias,
-    in_sem, send_sem, recv_sem, o_send_sem, o_recv_sem,
+    q_all, k_all, v_all, k_pack, v_pack, q_pack, k_got, v_got, q_got, o_send, t_bias,
+    in_sem, kv_send_sem, kv_recv_sem, q_send_sem, q_recv_sem, o_send_sem, o_recv_sem,
 ):
     me = lax.axis_index("seq")
     head = lax.axis_index("head")
-    z, y, c = me // (NY * NC), (me // NC) % NY, me % NC
-
-    def peer(i):
-        dz, dy, dc = (i * 3) % NZ, (i // NZ) % NY, i // (NZ * NY)
-        return ((z + dz) % NZ) * (NY * NC) + ((y + dy) % NY) * NC + (c + dc) % NC
-
-    for n, (src, dst) in enumerate(((q_hbm, q_all), (k_hbm, k_all), (v_hbm, v_all))):
+    z, y, c = lax.div(me, NY * NC), lax.rem(lax.div(me, NC), NY), lax.rem(me, NC)
+    z_part = [lax.rem(z + step, NZ) * (NY * NC) for step in (4, 3, 5, 2, 6, 1, 7, 0)]
+
+    def plane(i):
+        return lax.rem(y + lax.div(i, NC), NY) * NC + lax.rem(c + lax.rem(i, NC), NC)
+
+    def every_peer(act):
+        for part in z_part[:-1]:
+            act(part + y * NC + c)
+
+        def others(i, carry):
+            rest = plane(i)
+            for part in z_part:
+                act(part + rest)
+            return carry
+
+        lax.fori_loop(1, NY * NC, others, 0)
+
+    def load(n, src, dst):
         for j in range(LOCAL_HEADS):
             cols = pl.ds(j * HEAD_DIM, HEAD_DIM)
             pltpu.make_async_copy(src.at[:, cols], dst.at[j], in_sem.at[n]).start()
 
+    def loaded(n, dst):
+        pltpu.make_async_copy(dst, dst, in_sem.at[n]).wait()
+
+    def arrived(got, sem):
+        pltpu.make_async_copy(got, got, sem).wait()
+
+    def send_all(src, dst, mine, send_sem, recv_sem):
+        pltpu.make_async_copy(src(me), mine, recv_sem).start()
+
+        def send(other):
+            pltpu.make_async_remote_copy(
+                src_ref=src(other),
+                dst_ref=dst,
+                send_sem=send_sem,
+                recv_sem=recv_sem,
+                device_id=(other, head),
+                device_id_type=MESH,
+            ).start()
+
+        every_peer(send)
+
+    load(1, k_hbm, k_all)
+
     barrier = pltpu.get_barrier_semaphore()
-
-    def greet(i, carry):
-        pl.semaphore_signal(barrier, inc=1, device_id=(peer(i), head), device_id_type=MESH)
-        return carry
-
-    lax.fori_loop(1, SEQ, greet, 0)
+    for i in range(NY * NC):
+        rest = plane(i)
+        for part in z_part if i else z_part[:-1]:
+            pl.semaphore_signal(
+                barrier, inc=1, device_id=(part + rest, head), device_id_type=MESH
+            )
+
+    load(2, v_hbm, v_all)
+    load(0, q_hbm, q_all)
 
     ranks, count_t, count_s = [], jnp.int32(0), jnp.int32(HT_DEV)
     for j in range(LOCAL_HEADS):
@@ -82,37 +120,33 @@
             place = jnp.where(rank == n, j, place)
         return place
 
-    for n, whole in enumerate((q_all, k_all, v_all)):
-        pltpu.make_async_copy(whole, whole, in_sem.at[n]).wait()
-
-    def pack_head(t):
-        place = head_of(t)
-        for n, whole in enumerate((q_all, k_all, v_all)):
-            pack[t, :, n] = whole[place].reshape(SEQ, PIECE, HEAD_DIM)
-
-    def send_head(t):
-        pltpu.make_async_copy(pack.at[t, me], recv.at[t, me], recv_sem.at[t]).start()
-
-        def send(i, carry):
-            other = peer(i)
-            pltpu.make_async_remote_copy(
-                src_ref=pack.at[t, other],
-                dst_ref=recv.at[t, me],
-                send_sem=send_sem.at[t],
-                recv_sem=recv_sem.at[t],
-                device_id=(other, head),
-                device_id_type=MESH,
-            ).start()
-            return carry
-
-        lax.fori_loop(1, SEQ, send, 0)
-
-    pack_head(0)
+    places = [head_of(t) for t in range(HT_DEV)]
+
+    loaded(1, k_all)
+    for t, place in enumerate(places):
+        k_pack[:, t] = k_all[place].reshape(SEQ, PIECE, HEAD_DIM)
     pl.semaphore_wait(barrier, SEQ - 1)
-    send_head(0)
-    for t in range(1, HT_DEV):
-        pack_head(t)
-        send_head(t)
+    send_all(
+        lambda s: k_pack.at[s], k_got.at[me], k_got.at[me], kv_send_sem.at[0], kv_recv_sem.at[0]
+    )
+    loaded(2, v_all)
+    for t, place in enumerate(places):
+        v_pack[:, t] = v_all[place].reshape(SEQ, PIECE, HEAD_DIM)
+    send_all(
+        lambda s: v_pack.at[s], v_got.at[me], v_got.at[me], kv_send_sem.at[1], kv_recv_sem.at[1]
+    )
+    loaded(0, q_all)
+    for t, place in enumerate(places):
+        q_pack[t] = q_all[place].reshape(SEQ, PIECE, HEAD_DIM)
+
+    def send_queries(t, carry):
+        send_all(
+            lambda s: q_pack.at[t, s], q_got.at[t, me], q_got.at[t, me],
+            q_send_sem.at[t], q_recv_sem.at[t],
+        )
+        return carry
+
+    lax.fori_loop(0, HT_DEV, send_queries, 0)
 
     row = lax.broadcasted_iota(jnp.int32, (TILE, TILE), 0) % PIECE // 2
     col = lax.broadcasted_iota(jnp.int32, (TILE, TILE), 1) % PIECE // 2
@@ -144,48 +178,39 @@
 
     lax.fori_loop(0, HS_DEV, spatial_head, 0)
 
+    arrived(k_got, kv_recv_sem.at[0])
+    arrived(v_got, kv_recv_sem.at[1])
+
     def temporal_head(t, carry):
-        pltpu.make_async_copy(recv.at[t], recv.at[t], recv_sem.at[t]).wait()
+        arrived(q_got.at[t], q_recv_sem.at[t])
 
         def block(r, inner):
             frames = STEP // PIECE
             at = pl.ds(r * frames, frames)
             mixed = attend_rows(
-                recv[t, at, 0].reshape(STEP, HEAD_DIM),
-                recv[t, :, 1].reshape(ROWS, HEAD_DIM),
-                recv[t, :, 2].reshape(ROWS, HEAD_DIM),
+                q_got[t, at].reshape(STEP, HEAD_DIM),
+                k_got[:, t].reshape(ROWS, HEAD_DIM),
+                v_got[:, t].reshape(ROWS, HEAD_DIM),
                 lambda a, b: t_bias[...],
             )
             o_send[t, at] = mixed.reshape(frames, PIECE, HEAD_DIM)
             return inner
 
         lax.fori_loop(0, ROWS // STEP, block, 0)
-        mine = pl.ds(pl.multiple_of(me * PIECE, PIECE), PIECE)
-        pltpu.make_async_copy(o_send.at[t, me], out.at[t, mine], o_recv_sem.at[t]).start()
-
-        def send(i, inner):
-            other = peer(i)
-            pltpu.make_async_remote_copy(
-                src_ref=o_send.at[t, other],
-                dst_ref=out.at[t, mine],
-                send_sem=o_send_sem.at[t],
-                recv_sem=o_recv_sem.at[t],
-                device_id=(other, head),
-                device_id_type=MESH,
-            ).start()
-            return inner
-
-        lax.fori_loop(1, SEQ, send, 0)
+        mine = out.at[t, pl.ds(pl.multiple_of(me * PIECE, PIECE), PIECE)]
+        send_all(lambda s: o_send.at[t, s], mine, mine, o_send_sem.at[t], o_recv_sem.at[t])
         return carry
 
     lax.fori_loop(0, HT_DEV, temporal_head, 0)
 
+    others = pl.ds(0, SEQ - 1)
+    arrived(k_pack.at[others], kv_send_sem.at[0])
+    arrived(v_pack.at[others], kv_send_sem.at[1])
+
     def finish(t, carry):
-        sent = pack.at[t, pl.ds(0, SEQ - 1)]
-        pltpu.make_async_copy(sent, sent, send_sem.at[t]).wait()
-        sent = o_send.at[t, pl.ds(0, SEQ - 1)]
-        pltpu.make_async_copy(sent, sent, o_send_sem.at[t]).wait()
-        pltpu.make_async_copy(out.at[t], out.at[t], o_recv_sem.at[t]).wait()
+        arrived(q_pack.at[t, others], q_send_sem.at[t])
+        arrived(o_send.at[t, others], o_send_sem.at[t])
+        arrived(out.at[t], o_recv_sem.at[t])
         return carry
 
     lax.fori_loop(0, HT_DEV, finish, 0)
@@ -212,17 +237,20 @@
     smem = pl.BlockSpec(memory_space=pltpu.SMEM)
     anywhere = pl.BlockSpec(memory_space=pl.ANY)
     whole = pltpu.VMEM((LOCAL_HEADS, ROWS, HEAD_DIM), jnp.bfloat16)
-    moved = pltpu.VMEM((HT_DEV, SEQ, 3, PIECE, HEAD_DIM), jnp.bfloat16)
+    by_device = pltpu.VMEM((SEQ, HT_DEV, PIECE, HEAD_DIM), jnp.bfloat16)
+    by_head = pltpu.VMEM((HT_DEV, SEQ, PIECE, HEAD_DIM), jnp.bfloat16)
     packed = pl.pallas_call(
         main_kernel,
         out_shape=pltpu.VMEM((LOCAL_HEADS, ROWS, HEAD_DIM), jnp.bfloat16),
         in_specs=[smem] * 3 + [anywhere] * 3,
         out_specs=pl.BlockSpec(memory_space=pltpu.VMEM),
         scratch_shapes=[
-            whole, whole, whole, moved, moved,
-            pltpu.VMEM((HT_DEV, SEQ, PIECE, HEAD_DIM), jnp.bfloat16),
+            whole, whole, whole,
+            by_device, by_device, by_head, by_device, by_device, by_head, by_head,
             pltpu.VMEM((TILE, TILE), jnp.float32),
             pltpu.SemaphoreType.DMA((3,)),
+            pltpu.SemaphoreType.DMA((2,)),
+            pltpu.SemaphoreType.DMA((2,)),
             pltpu.SemaphoreType.DMA((HT_DEV,)),
             pltpu.SemaphoreType.DMA((HT_DEV,)),
             pltpu.SemaphoreType.DMA((HT_DEV,)),

time: 109 us -> 107 us (0.982)
  Pallas kernels: 109 us -> 107 us
    pallas_call x1, Pallas kernels: 107 us -> 105 us  [on_device(): pl.pallas_call(main_kernel, out_shape=pltpu.VMEM((LOCAL_HEADS, ROWS, HEAD...]
where the time goes in v4:
time: 107 us
  Pallas kernels  107 us (100%)
    pallas_call x1, Pallas kernels, on_device(): pl.pallas_call(main_kernel, out_shape=pltpu.VMEM((LOCAL_HEADS, ROWS, HEAD...  105 us

profile of v4, /device:TPU:1, one launch (start us, length us, event | category | flops | bytes accessed | tf_op | source)
XLA Modules:
  0.0 106.9 jit_solution(14640569026923060006)
XLA Ops:
  0.0 0.0 copy-start
  0.0 104.8 %attend_and_move.1.packed = bf16[10,1024,128]{2,1,0:T(8,128)(2,1)S(1)} custom-call(s32[10]{0:T(128)} %head_class.3, s32[1,8,8]{2,1,0:T(8,128)} %mask_s.1, s32[2,2,4]{2,1,0:T(2,128)} %bitcast.1, bf16[1024,1280]{1,0:T(8,128)(2,1)} %q_hbm.1, bf16[1024,1280]{1,0:T(8,128)(2,1)} %k_hbm.1, bf16[1024,1280]{1,0:T(8,128)(2,1)} %v_hbm.1), custom_call_target="tpu_custom_call" | custom-call | flops 5368709120 | bytes 10485760 | tf_op jit(solution)/shard_map/attend_and_move/pallas_call | solution.py:242
  104.8 0.0 copy-done
  104.8 2.1 %place_heads.1 = bf16[1024,1280]{1,0:T(8,128)(2,1)} custom-call(s32[10]{0:T(128)S(1)} %copy-done, bf16[10,1024,128]{2,1,0:T(8,128)(2,1)S(1)} %attend_and_move.1.packed), custom_call_target="tpu_custom_call" | custom-call | tf_op jit(solution)/shard_map/place_heads/pallas_call | solution.py:269
Async XLA Ops:
  0.0 104.8 %copy-start = (s32[10]{0:T(128)S(1)}, s32[10]{0:T(128)}, u32[]{:S(2)}) copy-start(s32[10]{0:T(128)} %head_class.3) | copy-start | bytes 124

commit v5 on v4

--- a/solution.py
+++ b/solution.py
@@ -44,9 +44,9 @@
 
 
 def main_kernel(
-    head_class, mask_s, mask_t, q_hbm, k_hbm, v_hbm, out,
-    q_all, k_all, v_all, k_pack, v_pack, q_pack, k_got, v_got, q_got, o_send, t_bias,
-    in_sem, kv_send_sem, kv_recv_sem, q_send_sem, q_recv_sem, o_send_sem, o_recv_sem,
+    head_class_hbm, mask_s_hbm, mask_t_hbm, q_hbm, k_hbm, v_hbm, out,
+    head_class, mask_s, mask_t, q_all, k_all, v_all, k_pack, v_pack, q_pack, k_got, v_got, q_got, o_send, t_bias,
+    small_sem, in_sem, plane_sem, kv_send_sem, kv_recv_sem, q_send_sem, q_recv_sem, o_send_sem, o_recv_sem,
 ):
     me = lax.axis_index("seq")
     head = lax.axis_index("head")
@@ -56,13 +56,13 @@
     def plane(i):
         return lax.rem(y + lax.div(i, NC), NY) * NC + lax.rem(c + lax.rem(i, NC), NC)
 
-    def every_peer(act):
-        for part in z_part[:-1]:
-            act(part + y * NC + c)
-
+    own_plane = [z_part[-1] + plane(i) for i in range(1, NY * NC)]
+    near = [part + y * NC + c for part in z_part[:-1]] + own_plane
+
+    def far_peers(act):
         def others(i, carry):
             rest = plane(i)
-            for part in z_part:
+            for part in z_part[:-1]:
                 act(part + rest)
             return carry
 
@@ -79,7 +79,7 @@
     def arrived(got, sem):
         pltpu.make_async_copy(got, got, sem).wait()
 
-    def send_all(src, dst, mine, send_sem, recv_sem):
+    def send_all(src, dst, mine, send_sem, recv_sem, between=lambda: None):
         pltpu.make_async_copy(src(me), mine, recv_sem).start()
 
         def send(other):
@@ -92,20 +92,26 @@
                 device_id_type=MESH,
             ).start()
 
-        every_peer(send)
-
+        for other in near:
+            send(other)
+        between()
+        far_peers(send)
+
+    smalls = [
+        pltpu.make_async_copy(src, dst, small_sem.at[n])
+        for n, (src, dst) in enumerate(
+            ((head_class_hbm, head_class), (mask_s_hbm, mask_s), (mask_t_hbm, mask_t))
+        )
+    ]
+    smalls[0].start()
     load(1, k_hbm, k_all)
 
     barrier = pltpu.get_barrier_semaphore()
-    for i in range(NY * NC):
-        rest = plane(i)
-        for part in z_part if i else z_part[:-1]:
-            pl.semaphore_signal(
-                barrier, inc=1, device_id=(part + rest, head), device_id_type=MESH
-            )
-
-    load(2, v_hbm, v_all)
-    load(0, q_hbm, q_all)
+    for other in near:
+        pl.semaphore_signal(barrier, inc=1, device_id=(other, head), device_id_type=MESH)
+    for small in smalls[1:]:
+        small.start()
+    smalls[0].wait()
 
     ranks, count_t, count_s = [], jnp.int32(0), jnp.int32(HT_DEV)
     for j in range(LOCAL_HEADS):
@@ -122,13 +128,19 @@
 
     places = [head_of(t) for t in range(HT_DEV)]
 
+    pl.semaphore_wait(barrier, len(near))
+    for other in own_plane:
+        pl.semaphore_signal(plane_sem, inc=1, device_id=(other, head), device_id_type=MESH)
+
     loaded(1, k_all)
     for t, place in enumerate(places):
         k_pack[:, t] = k_all[place].reshape(SEQ, PIECE, HEAD_DIM)
-    pl.semaphore_wait(barrier, SEQ - 1)
     send_all(
-        lambda s: k_pack.at[s], k_got.at[me], k_got.at[me], kv_send_sem.at[0], kv_recv_sem.at[0]
+        lambda s: k_pack.at[s], k_got.at[me], k_got.at[me], kv_send_sem.at[0], kv_recv_sem.at[0],
+        between=lambda: pl.semaphore_wait(plane_sem, len(own_plane)),
     )
+    load(2, v_hbm, v_all)
+    load(0, q_hbm, q_all)
     loaded(2, v_all)
     for t, place in enumerate(places):
         v_pack[:, t] = v_all[place].reshape(SEQ, PIECE, HEAD_DIM)
@@ -148,6 +160,8 @@
 
     lax.fori_loop(0, HT_DEV, send_queries, 0)
 
+    for small in smalls[1:]:
+        small.wait()
     row = lax.broadcasted_iota(jnp.int32, (TILE, TILE), 0) % PIECE // 2
     col = lax.broadcasted_iota(jnp.int32, (TILE, TILE), 1) % PIECE // 2
     bias = jnp.full((TILE, TILE), NEG, jnp.float32)
@@ -242,13 +256,18 @@
     packed = pl.pallas_call(
         main_kernel,
         out_shape=pltpu.VMEM((LOCAL_HEADS, ROWS, HEAD_DIM), jnp.bfloat16),
-        in_specs=[smem] * 3 + [anywhere] * 3,
+        in_specs=[anywhere] * 6,
         out_specs=pl.BlockSpec(memory_space=pltpu.VMEM),
         scratch_shapes=[
+            pltpu.SMEM(head_class.shape, jnp.int32),
+            pltpu.SMEM(mask_spatial.shape, jnp.int32),
+            pltpu.SMEM(mask_temporal.shape[1:] + mask_temporal.shape[:1], jnp.int32),
             whole, whole, whole,
             by_device, by_device, by_head, by_device, by_device, by_head, by_head,
             pltpu.VMEM((TILE, TILE), jnp.float32),
             pltpu.SemaphoreType.DMA((3,)),
+            pltpu.SemaphoreType.DMA((3,)),
+            pltpu.SemaphoreType.REGULAR,
             pltpu.SemaphoreType.DMA((2,)),
             pltpu.SemaphoreType.DMA((2,)),
             pltpu.SemaphoreType.DMA((HT_DEV,)),

time: 107 us -> 105 us (0.981)
  Pallas kernels: 107 us -> 105 us
    pallas_call x1, Pallas kernels: 105 us -> 102 us  [on_device(): pl.pallas_call(main_kernel, out_shape=pltpu.VMEM((LOCAL_HEADS, ROWS, HEAD...]
where the time goes in v5:
time: 105 us
  Pallas kernels  105 us (100%)
    pallas_call x1, Pallas kernels, on_device(): pl.pallas_call(main_kernel, out_shape=pltpu.VMEM((LOCAL_HEADS, ROWS, HEAD...  102 us
    pallas_call x1, Pallas kernels, on_device(): pl.pallas_call(place_kernel, out_shape=jax.ShapeDtypeStruct((ROWS, LOCAL_...  2.11 us

profile of v5, /device:TPU:1, one launch (start us, length us, event | category | flops | bytes accessed | tf_op | source)
XLA Modules:
  0.0 104.5 jit_solution(13324179403954919248)
XLA Ops:
  0.0 0.0 copy-start
  0.0 102.4 %attend_and_move.1.packed = bf16[10,1024,128]{2,1,0:T(8,128)(2,1)S(1)} custom-call(s32[10]{0:T(128)} %head_class.1, s32[1,8,8]{2,1,0:T(8,128)} %mask_s_hbm.1, s32[2,2,4]{2,1,0:T(2,128)} %bitcast.1, bf16[1024,1280]{1,0:T(8,128)(2,1)} %q_hbm.1, bf16[1024,1280]{1,0:T(8,128)(2,1)} %k_hbm.1, bf16[1024,1280]{1,0:T(8,128)(2,1)} %v_hbm.1), custom_call_target="tpu_custom_call" | custom-call | flops 5368709120 | bytes 10485760 | tf_op jit(solution)/shard_map/attend_and_move/pallas_call | solution.py:256
  102.4 0.0 copy-done
  102.4 2.1 %place_heads.1 = bf16[1024,1280]{1,0:T(8,128)(2,1)} custom-call(s32[10]{0:T(128)S(1)} %copy-done, bf16[10,1024,128]{2,1,0:T(8,128)(2,1)S(1)} %attend_and_move.1.packed), custom_call_target="tpu_custom_call" | custom-call | tf_op jit(solution)/shard_map/place_heads/pallas_call | solution.py:288
Async XLA Ops:
  0.0 102.4 %copy-start = (s32[10]{0:T(128)S(1)}, s32[10]{0:T(128)}, u32[]{:S(2)}) copy-start(s32[10]{0:T(128)} %head_class.1) | copy-start | bytes 124

commit v6 on v5

--- a/solution.py
+++ b/solution.py
@@ -79,7 +79,22 @@
     def arrived(got, sem):
         pltpu.make_async_copy(got, got, sem).wait()
 
-    def send_all(src, dst, mine, send_sem, recv_sem, between=lambda: None):
+    def by_place(act):
+        def one_plane(k, carry):
+            for i in range(NY * NC):
+                other = k * (NY * NC) + plane(i)
+                pl.when(other != me)(functools.partial(act, other))
+            return carry
+
+        lax.fori_loop(0, NZ, one_plane, 0)
+
+    def near_first(act, between=lambda: None):
+        for other in near:
+            act(other)
+        between()
+        far_peers(act)
+
+    def send_all(src, dst, mine, send_sem, recv_sem, order=near_first):
         pltpu.make_async_copy(src(me), mine, recv_sem).start()
 
         def send(other):
@@ -92,10 +107,7 @@
                 device_id_type=MESH,
             ).start()
 
-        for other in near:
-            send(other)
-        between()
-        far_peers(send)
+        order(send)
 
     smalls = [
         pltpu.make_async_copy(src, dst, small_sem.at[n])
@@ -137,7 +149,9 @@
         k_pack[:, t] = k_all[place].reshape(SEQ, PIECE, HEAD_DIM)
     send_all(
         lambda s: k_pack.at[s], k_got.at[me], k_got.at[me], kv_send_sem.at[0], kv_recv_sem.at[0],
-        between=lambda: pl.semaphore_wait(plane_sem, len(own_plane)),
+        functools.partial(
+            near_first, between=lambda: pl.semaphore_wait(plane_sem, len(own_plane))
+        ),
     )
     load(2, v_hbm, v_all)
     load(0, q_hbm, q_all)
@@ -212,7 +226,9 @@
 
         lax.fori_loop(0, ROWS // STEP, block, 0)
         mine = out.at[t, pl.ds(pl.multiple_of(me * PIECE, PIECE), PIECE)]
-        send_all(lambda s: o_send.at[t, s], mine, mine, o_send_sem.at[t], o_recv_sem.at[t])
+        send_all(
+            lambda s: o_send.at[t, s], mine, mine, o_send_sem.at[t], o_recv_sem.at[t], by_place
+        )
         return carry
 
     lax.fori_loop(0, HT_DEV, temporal_head, 0)

time: 105 us -> 103 us (0.981)
  Pallas kernels: 105 us -> 103 us
    pallas_call x1, Pallas kernels: 102 us -> 101 us  [on_device(): pl.pallas_call(main_kernel, out_shape=pltpu.VMEM((LOCAL_HEADS, ROWS, HEAD...]
where the time goes in v6:
time: 103 us
  Pallas kernels  103 us (100%)
    pallas_call x1, Pallas kernels, on_device(): pl.pallas_call(main_kernel, out_shape=pltpu.VMEM((LOCAL_HEADS, ROWS, HEAD...  101 us
    pallas_call x1, Pallas kernels, on_device(): pl.pallas_call(place_kernel, out_shape=jax.ShapeDtypeStruct((ROWS, LOCAL_...  2.11 us

profile of v6, /device:TPU:1, one launch (start us, length us, event | category | flops | bytes accessed | tf_op | source)
XLA Modules:
  0.0 102.7 jit_solution(7208091158447482476)
XLA Ops:
  0.0 0.0 copy-start
  0.0 100.6 %attend_and_move.1.packed = bf16[10,1024,128]{2,1,0:T(8,128)(2,1)S(1)} custom-call(s32[10]{0:T(128)} %head_class.1, s32[1,8,8]{2,1,0:T(8,128)} %mask_s_hbm.1, s32[2,2,4]{2,1,0:T(2,128)} %bitcast.1, bf16[1024,1280]{1,0:T(8,128)(2,1)} %q_hbm.1, bf16[1024,1280]{1,0:T(8,128)(2,1)} %k_hbm.1, bf16[1024,1280]{1,0:T(8,128)(2,1)} %v_hbm.1), custom_call_target="tpu_custom_call" | custom-call | flops 5368709120 | bytes 10485760 | tf_op jit(solution)/shard_map/attend_and_move/pallas_call | solution.py:272
  100.6 0.0 copy-done
  100.6 2.1 %place_heads.1 = bf16[1024,1280]{1,0:T(8,128)(2,1)} custom-call(s32[10]{0:T(128)S(1)} %copy-done, bf16[10,1024,128]{2,1,0:T(8,128)(2,1)S(1)} %attend_and_move.1.packed), custom_call_target="tpu_custom_call" | custom-call | tf_op jit(solution)/shard_map/place_heads/pallas_call | solution.py:304
Async XLA Ops:
  0.0 100.6 %copy-start = (s32[10]{0:T(128)S(1)}, s32[10]{0:T(128)}, u32[]{:S(2)}) copy-start(s32[10]{0:T(128)} %head_class.1) | copy-start | bytes 124

commit v7 on v6

--- a/solution.py
+++ b/solution.py
@@ -79,10 +79,10 @@
     def arrived(got, sem):
         pltpu.make_async_copy(got, got, sem).wait()
 
-    def by_place(act):
+    def by_index(act):
         def one_plane(k, carry):
             for i in range(NY * NC):
-                other = k * (NY * NC) + plane(i)
+                other = k * (NY * NC) + i
                 pl.when(other != me)(functools.partial(act, other))
             return carry
 
@@ -227,7 +227,7 @@
         lax.fori_loop(0, ROWS // STEP, block, 0)
         mine = out.at[t, pl.ds(pl.multiple_of(me * PIECE, PIECE), PIECE)]
         send_all(
-            lambda s: o_send.at[t, s], mine, mine, o_send_sem.at[t], o_recv_sem.at[t], by_place
+            lambda s: o_send.at[t, s], mine, mine, o_send_sem.at[t], o_recv_sem.at[t], by_index
         )
         return carry
 

time: 103 us -> 102 us (level)
  no operation moved by 1% of the time
where the time goes in v7:
time: 102 us
  Pallas kernels  102 us (100%)
    pallas_call x1, Pallas kernels, on_device(): pl.pallas_call(main_kernel, out_shape=pltpu.VMEM((LOCAL_HEADS, ROWS, HEAD...  99.6 us
    pallas_call x1, Pallas kernels, on_device(): pl.pallas_call(place_kernel, out_shape=jax.ShapeDtypeStruct((ROWS, LOCAL_...  2.11 us

profile of v7, /device:TPU:1, one launch (start us, length us, event | category | flops | bytes accessed | tf_op | source)
XLA Modules:
  0.0 101.8 jit_solution(1065958343042761585)
XLA Ops:
  0.0 0.0 copy-start
  0.0 99.6 %attend_and_move.1.packed = bf16[10,1024,128]{2,1,0:T(8,128)(2,1)S(1)} custom-call(s32[10]{0:T(128)} %head_class.1, s32[1,8,8]{2,1,0:T(8,128)} %mask_s_hbm.1, s32[2,2,4]{2,1,0:T(2,128)} %bitcast.1, bf16[1024,1280]{1,0:T(8,128)(2,1)} %q_hbm.1, bf16[1024,1280]{1,0:T(8,128)(2,1)} %k_hbm.1, bf16[1024,1280]{1,0:T(8,128)(2,1)} %v_hbm.1), custom_call_target="tpu_custom_call" | custom-call | flops 5368709120 | bytes 10485760 | tf_op jit(solution)/shard_map/attend_and_move/pallas_call | solution.py:272
  99.6 0.0 copy-done
  99.6 2.1 %place_heads.1 = bf16[1024,1280]{1,0:T(8,128)(2,1)} custom-call(s32[10]{0:T(128)S(1)} %copy-done, bf16[10,1024,128]{2,1,0:T(8,128)(2,1)S(1)} %attend_and_move.1.packed), custom_call_target="tpu_custom_call" | custom-call | tf_op jit(solution)/shard_map/place_heads/pallas_call | solution.py:304
Async XLA Ops:
  0.0 99.6 %copy-start = (s32[10]{0:T(128)S(1)}, s32[10]{0:T(128)}, u32[]{:S(2)}) copy-start(s32[10]{0:T(128)} %head_class.1) | copy-start | bytes 124

commit v8 on v7

--- a/solution.py
+++ b/solution.py
@@ -17,6 +17,7 @@
 SEQ = 64
 PIECE = ROWS // SEQ
 NZ, NY, NC = 8, 4, 2
+PLANE = ROWS // NZ
 STEP = 256
 EXP_SCALE = HEAD_DIM**-0.5 * math.log2(math.e)
 NEG = -1e30
@@ -45,7 +46,7 @@
 
 def main_kernel(
     head_class_hbm, mask_s_hbm, mask_t_hbm, q_hbm, k_hbm, v_hbm, out,
-    head_class, mask_s, mask_t, q_all, k_all, v_all, k_pack, v_pack, q_pack, k_got, v_got, q_got, o_send, t_bias,
+    head_class, mask_s, mask_t, q_all, k_all, v_all, k_pack, v_pack, q_pack, k_got, v_got, q_got, o_send, s_done, t_done, t_bias,
     small_sem, in_sem, plane_sem, kv_send_sem, kv_recv_sem, q_send_sem, q_recv_sem, o_send_sem, o_recv_sem,
 ):
     me = lax.axis_index("seq")
@@ -196,7 +197,7 @@
                 allowed = mask_s[0, r * (STEP // TILE) + a, b] > 0
                 return jnp.where(allowed, 0.0, NEG).astype(jnp.float32)
 
-            out[HT_DEV + n, pl.ds(at, STEP)] = attend_rows(
+            s_done[n, pl.ds(at, STEP)] = attend_rows(
                 q_all[place, pl.ds(at, STEP)], k_all[place], v_all[place], tile_bias
             )
             return inner
@@ -205,6 +206,8 @@
         return carry
 
     lax.fori_loop(0, HS_DEV, spatial_head, 0)
+    for j, rank in enumerate(ranks):
+        out[:, j * HEAD_DIM : (j + 1) * HEAD_DIM] = s_done[jnp.clip(rank - HT_DEV, 0, HS_DEV - 1)]
 
     arrived(k_got, kv_recv_sem.at[0])
     arrived(v_got, kv_recv_sem.at[1])
@@ -225,9 +228,9 @@
             return inner
 
         lax.fori_loop(0, ROWS // STEP, block, 0)
-        mine = out.at[t, pl.ds(pl.multiple_of(me * PIECE, PIECE), PIECE)]
+        mine = t_done.at[t, pl.ds(pl.multiple_of(me * PIECE, PIECE), PIECE)]
         send_all(
-            lambda s: o_send.at[t, s], mine, mine, o_send_sem.at[t], o_recv_sem.at[t], by_index
+            lambda s: o_send.at[t, s], mine, mine, o_send_sem.at[t], o_recv_sem.at[t, z], by_index
         )
         return carry
 
@@ -237,30 +240,23 @@
     arrived(k_pack.at[others], kv_send_sem.at[0])
     arrived(v_pack.at[others], kv_send_sem.at[1])
 
-    def finish(t, carry):
+    def place(t):
+        def one_plane(i, carry):
+            step = (1 - 2 * lax.rem(i, 2)) * lax.div(i + 1, 2)
+            k = lax.rem(z + NZ + step, NZ)
+            at = pl.ds(pl.multiple_of(k * PLANE, PLANE), PLANE)
+            arrived(t_done.at[t, at], o_recv_sem.at[t, k])
+            for j in range(t, t + HS_DEV + 1):
+                cols = pl.ds(j * HEAD_DIM, HEAD_DIM)
+                out[at, cols] = jnp.where(ranks[j] == t, t_done[t, at], out[at, cols])
+            return carry
+
+        lax.fori_loop(0, NZ, one_plane, 0)
+
+    for t in range(HT_DEV):
         arrived(q_pack.at[t, others], q_send_sem.at[t])
+        place(t)
         arrived(o_send.at[t, others], o_send_sem.at[t])
-        arrived(out.at[t], o_recv_sem.at[t])
-        return carry
-
-    lax.fori_loop(0, HT_DEV, finish, 0)
-
-
-def place_kernel(head_class, packed, out, sem):
-    count_t, count_s = jnp.int32(0), jnp.int32(HT_DEV)
-    copies = []
-    for j in range(LOCAL_HEADS):
-        is_t = head_class[j] > 0
-        rank = jnp.where(is_t, count_t, count_s)
-        count_t = count_t + jnp.where(is_t, 1, 0)
-        count_s = count_s + jnp.where(is_t, 0, 1)
-        copy = pltpu.make_async_copy(
-            packed.at[rank], out.at[:, pl.ds(j * HEAD_DIM, HEAD_DIM)], sem.at[j]
-        )
-        copy.start()
-        copies.append(copy)
-    for copy in copies:
-        copy.wait()
 
 
 def on_device(queries, keys, values, head_class, mask_spatial, mask_temporal):
@@ -269,9 +265,9 @@
     whole = pltpu.VMEM((LOCAL_HEADS, ROWS, HEAD_DIM), jnp.bfloat16)
     by_device = pltpu.VMEM((SEQ, HT_DEV, PIECE, HEAD_DIM), jnp.bfloat16)
     by_head = pltpu.VMEM((HT_DEV, SEQ, PIECE, HEAD_DIM), jnp.bfloat16)
-    packed = pl.pallas_call(
+    return pl.pallas_call(
         main_kernel,
-        out_shape=pltpu.VMEM((LOCAL_HEADS, ROWS, HEAD_DIM), jnp.bfloat16),
+        out_shape=pltpu.VMEM((ROWS, LOCAL_HEADS * HEAD_DIM), jnp.bfloat16),
         in_specs=[anywhere] * 6,
         out_specs=pl.BlockSpec(memory_space=pltpu.VMEM),
         scratch_shapes=[
@@ -280,6 +276,8 @@
             pltpu.SMEM(mask_temporal.shape[1:] + mask_temporal.shape[:1], jnp.int32),
             whole, whole, whole,
             by_device, by_device, by_head, by_device, by_device, by_head, by_head,
+            pltpu.VMEM((HS_DEV, ROWS, HEAD_DIM), jnp.bfloat16),
+            pltpu.VMEM((HT_DEV, ROWS, HEAD_DIM), jnp.bfloat16),
             pltpu.VMEM((TILE, TILE), jnp.float32),
             pltpu.SemaphoreType.DMA((3,)),
             pltpu.SemaphoreType.DMA((3,)),
@@ -289,7 +287,7 @@
             pltpu.SemaphoreType.DMA((HT_DEV,)),
             pltpu.SemaphoreType.DMA((HT_DEV,)),
             pltpu.SemaphoreType.DMA((HT_DEV,)),
-            pltpu.SemaphoreType.DMA((HT_DEV,)),
+            pltpu.SemaphoreType.DMA((HT_DEV, NZ)),
         ],
         compiler_params=pltpu.CompilerParams(
             collective_id=0, has_side_effects=True, vmem_limit_bytes=60 << 20
@@ -301,15 +299,6 @@
         ),
         name="attend_and_move",
     )(head_class, mask_spatial, jnp.transpose(mask_temporal, (1, 2, 0)), queries, keys, values)
-    return pl.pallas_call(
-        place_kernel,
-        out_shape=jax.ShapeDtypeStruct((ROWS, LOCAL_HEADS * HEAD_DIM), jnp.bfloat16),
-        in_specs=[smem, anywhere],
-        out_specs=anywhere,
-        scratch_shapes=[pltpu.SemaphoreType.DMA((LOCAL_HEADS,))],
-        compiler_params=pltpu.CompilerParams(vmem_limit_bytes=8 << 20),
-        name="place_heads",
-    )(head_class, pltpu.with_memory_space_constraint(packed, pltpu.VMEM))
 
 
 def solution(mesh):

time: 102 us -> 102 us (level)
  Pallas kernels: 102 us -> 100 us
  local copies, waits for them, and re-layouts: 0.01 us -> 1.49 us
    pallas_call x2 -> x1, Pallas kernels: 102 us -> 100 us  [on_device(): pl.pallas_call(main_kernel, out_shape=pltpu.VMEM((ROWS, LOCAL_HEADS * HEA...]
    unnamed x2 -> x1, local copies, waits for them, and re-layouts: 0.01 us -> 1.49 us
where the time goes in v8:
time: 102 us; the launch traced here: 101 us
  Pallas kernels  100 us (98%)
  local copies, waits for them, and re-layouts  1.49 us (1%)
    pallas_call x1, Pallas kernels, on_device(): pl.pallas_call(main_kernel, out_shape=pltpu.VMEM((ROWS, LOCAL_HEADS * HEA...  100 us

profile of v8, /device:TPU:1, one launch (start us, length us, event | category | flops | bytes accessed | tf_op | source)
XLA Modules:
  0.0 101.5 jit_solution(18185019657374274697)
XLA Ops:
  0.0 100.0 %attend_and_move.1 = bf16[1024,1280]{1,0:T(8,128)(2,1)S(1)} custom-call(s32[10]{0:T(128)} %head_class_hbm.1, s32[1,8,8]{2,1,0:T(8,128)} %mask_s_hbm.1, s32[2,2,4]{2,1,0:T(2,128)} %bitcast.1, bf16[1024,1280]{1,0:T(8,128)(2,1)} %q_hbm.1, bf16[1024,1280]{1,0:T(8,128)(2,1)} %k_hbm.1, bf16[1024,1280]{1,0:T(8,128)(2,1)} %v_hbm.1), custom_call_target="tpu_custom_call" | custom-call | flops 5368709120 | bytes 10485760 | tf_op jit(solution)/shard_map/attend_and_move/pallas_call | solution.py:268
  100.0 1.5 %copy.8 = bf16[1024,1280]{1,0:T(8,128)(2,1)} copy(bf16[1024,1280]{1,0:T(8,128)(2,1)S(1)} %attend_and_move.1) | data formatting | bytes 5242880

commit v9 on v7

--- a/solution.py
+++ b/solution.py
@@ -225,13 +225,34 @@
             return inner
 
         lax.fori_loop(0, ROWS // STEP, block, 0)
-        mine = out.at[t, pl.ds(pl.multiple_of(me * PIECE, PIECE), PIECE)]
-        send_all(
-            lambda s: o_send.at[t, s], mine, mine, o_send_sem.at[t], o_recv_sem.at[t], by_index
-        )
-        return carry
-
-    lax.fori_loop(0, HT_DEV, temporal_head, 0)
+        return carry
+
+    def return_heads(heads):
+        at = pl.ds(pl.multiple_of(me * PIECE, PIECE), PIECE)
+        for t in heads:
+            pltpu.make_async_copy(o_send.at[t, me], out.at[t, at], o_recv_sem.at[t]).start()
+
+        def send(other):
+            for t in heads:
+                pltpu.make_async_remote_copy(
+                    src_ref=o_send.at[t, other],
+                    dst_ref=out.at[t, at],
+                    send_sem=o_send_sem.at[t],
+                    recv_sem=o_recv_sem.at[t],
+                    device_id=(other, head),
+                    device_id_type=MESH,
+                ).start()
+
+        by_index(send)
+
+    def early_head(t, carry):
+        temporal_head(t, carry)
+        return_heads((t,))
+        return carry
+
+    lax.fori_loop(0, HT_DEV - 2, early_head, 0)
+    lax.fori_loop(HT_DEV - 2, HT_DEV, temporal_head, 0)
+    return_heads((HT_DEV - 2, HT_DEV - 1))
 
     others = pl.ds(0, SEQ - 1)
     arrived(k_pack.at[others], kv_send_sem.at[0])

time: 102 us -> 102 us (level)
  the two profiles are of different devices: /device:TPU:1 before, /device:TPU:91 now
where the time goes in v9:
time: 102 us
  Pallas kernels  102 us (100%)
    pallas_call x1, Pallas kernels, on_device(): pl.pallas_call(main_kernel, out_shape=pltpu.VMEM((LOCAL_HEADS, ROWS, HEAD...  99.5 us
    pallas_call x1, Pallas kernels, on_device(): pl.pallas_call(place_kernel, out_shape=jax.ShapeDtypeStruct((ROWS, LOCAL_...  2.11 us

profile of v9, /device:TPU:91, one launch (start us, length us, event | category | flops | bytes accessed | tf_op | source)
XLA Modules:
  0.0 101.6 jit_solution(3846547197051610087)
XLA Ops:
  0.0 0.0 copy-start
  0.0 99.5 %attend_and_move.1.packed = bf16[10,1024,128]{2,1,0:T(8,128)(2,1)S(1)} custom-call(s32[10]{0:T(128)} %head_class.1, s32[1,8,8]{2,1,0:T(8,128)} %mask_s_hbm.1, s32[2,2,4]{2,1,0:T(2,128)} %bitcast.1, bf16[1024,1280]{1,0:T(8,128)(2,1)} %q_hbm.1, bf16[1024,1280]{1,0:T(8,128)(2,1)} %k_hbm.1, bf16[1024,1280]{1,0:T(8,128)(2,1)} %v_hbm.1), custom_call_target="tpu_custom_call" | custom-call | flops 5368709120 | bytes 10485760 | tf_op jit(solution)/shard_map/attend_and_move/pallas_call | solution.py:293
  99.5 0.0 copy-done
  99.5 2.1 %place_heads.1 = bf16[1024,1280]{1,0:T(8,128)(2,1)} custom-call(s32[10]{0:T(128)S(1)} %copy-done, bf16[10,1024,128]{2,1,0:T(8,128)(2,1)S(1)} %attend_and_move.1.packed), custom_call_target="tpu_custom_call" | custom-call | tf_op jit(solution)/shard_map/place_heads/pallas_call | solution.py:325
Async XLA Ops:
  0.0 99.5 %copy-start = (s32[10]{0:T(128)S(1)}, s32[10]{0:T(128)}, u32[]{:S(2)}) copy-start(s32[10]{0:T(128)} %head_class.1) | copy-start | bytes 124

commit v10 on v9

--- a/solution.py
+++ b/solution.py
@@ -243,7 +243,13 @@
                     device_id_type=MESH,
                 ).start()
 
-        by_index(send)
+        if len(heads) == 1:
+            by_index(send)
+            return
+        size = NY * NC
+        mixed = [k * size + i for i in range(size) for k in (2, 1)]
+        for other in [*range(size), *mixed, *range(3 * size, SEQ)]:
+            pl.when(other != me)(functools.partial(send, other))
 
     def early_head(t, carry):
         temporal_head(t, carry)

time: 102 us -> 102 us (level)
  the two profiles are of different devices: /device:TPU:91 before, /device:TPU:57 now
where the time goes in v10:
time: 102 us
  Pallas kernels  102 us (100%)
    pallas_call x1, Pallas kernels, on_device(): pl.pallas_call(main_kernel, out_shape=pltpu.VMEM((LOCAL_HEADS, ROWS, HEAD...  99.9 us
    pallas_call x1, Pallas kernels, on_device(): pl.pallas_call(place_kernel, out_shape=jax.ShapeDtypeStruct((ROWS, LOCAL_...  2.11 us

profile of v10, /device:TPU:57, one launch (start us, length us, event | category | flops | bytes accessed | tf_op | source)
XLA Modules:
  0.0 102.0 jit_solution(4839680239601515241)
XLA Ops:
  0.0 0.0 copy-start
  0.0 99.9 %attend_and_move.1.packed = bf16[10,1024,128]{2,1,0:T(8,128)(2,1)S(1)} custom-call(s32[10]{0:T(128)} %head_class.1, s32[1,8,8]{2,1,0:T(8,128)} %mask_s_hbm.1, s32[2,2,4]{2,1,0:T(2,128)} %bitcast.1, bf16[1024,1280]{1,0:T(8,128)(2,1)} %q_hbm.1, bf16[1024,1280]{1,0:T(8,128)(2,1)} %k_hbm.1, bf16[1024,1280]{1,0:T(8,128)(2,1)} %v_hbm.1), custom_call_target="tpu_custom_call" | custom-call | flops 5368709120 | bytes 10485760 | tf_op jit(solution)/shard_map/attend_and_move/pallas_call | solution.py:299
  99.9 0.0 copy-done
  99.9 2.1 %place_heads.1 = bf16[1024,1280]{1,0:T(8,128)(2,1)} custom-call(s32[10]{0:T(128)S(1)} %copy-done, bf16[10,1024,128]{2,1,0:T(8,128)(2,1)S(1)} %attend_and_move.1.packed), custom_call_target="tpu_custom_call" | custom-call | tf_op jit(solution)/shard_map/place_heads/pallas_call | solution.py:331
Async XLA Ops:
  0.0 99.9 %copy-start = (s32[10]{0:T(128)S(1)}, s32[10]{0:T(128)}, u32[]{:S(2)}) copy-start(s32[10]{0:T(128)} %head_class.1) | copy-start | bytes 124
